TPU v7x, 256 devices: a whole 4x4x8 slice. The times are simulated.
256 devices in a mesh: group: 4 (over x), within: 64 (over z, y, core).
Axes of the slice: x: 4, y: 4, z: 8, core: 2. Of those that a mesh axis runs over, the one named last changes fastest.
Arguments:
- coords: float32 [1048576, 64], P(('group', 'within')), may hold values from -6 to 6
- perm: int32 [1048576], P(('group', 'within')), may hold values from 0 to 4095, as said below
- inv_scale: float32 [64], replicated, may hold values from 0.08 to 0.4
- noise: float32 [1], replicated, may hold values from 0.1 to 1
- leaf_basis: float32 [1048576, 64], P(('group', 'within')), may hold values from -0.25 to 0.25
- pair_transfer: float32 [2048, 64, 128], P(('group', 'within')), may hold values from -0.5 to 0.5
- coupling: float32 [2048, 64, 64], P(('group', 'within')), may hold values from -0.75 to 0.75
- solution: float32 [1048576, 64], P(('group', 'within')), may hold values from -6 to 6
- residual: float32 [1048576, 64], P(('group', 'within')), may hold values from -6 to 6
- direction: float32 [1048576, 64], P(('group', 'within')), may hold values from -6 to 6
Outputs:
- new_solution: float32 [1048576, 64], P(('group', 'within'))
- new_residual: float32 [1048576, 64], P(('group', 'within'))
- new_direction: float32 [1048576, 64], P(('group', 'within'))
Inputs may be any that keep to these rules, and one draw needn't show every extreme that they name: `perm`: each aligned block of 4096 entries holds every number from 0 to 4095 exactly once.
All inputs are finite; a program needn't handle non-finite values.
Results may differ from a plain program's by a relative error of at most 0.00012.
Values sent between devices are 32-bit elements; how exact they have to be, the bound alone decides.
A program may use at most 128 MiB of HBM per device.

v0:
```python
import math

import jax
import jax.numpy as jnp
from jax import lax
from jax.sharding import PartitionSpec as P

LEAF = 512


HIGH = lax.Precision.HIGHEST
ROOT_FIVE = math.sqrt(5.0)


def matern_block(scaled):
    squares = jnp.sum(scaled * scaled, axis=1)
    inner = jnp.dot(scaled, scaled.T, precision=HIGH)
    dist_sq = jnp.maximum(squares[:, None] + squares[None, :] - 2.0 * inner, 0.0)
    dist = jnp.sqrt(dist_sq)
    return (1.0 + ROOT_FIVE * dist + 5.0 / 3.0 * dist_sq) * jnp.exp(-ROOT_FIVE * dist)


def leaf_product(item):
    return jnp.dot(matern_block(item[0]), item[1], precision=HIGH)


def raise_pair(transfer, left, right):
    width = left.shape[1]
    upper = jnp.einsum("kab,kan->kbn", transfer[:, :, :width], left, precision=HIGH)
    return upper + jnp.einsum("kab,kan->kbn", transfer[:, :, width:], right, precision=HIGH)


def lower_pair(transfer, couple, left, right, parent):
    width = left.shape[1]
    f_left = jnp.einsum("kab,kbn->kan", couple, right, precision=HIGH) + jnp.einsum(
        "kab,kbn->kan", transfer[:, :, :width], parent, precision=HIGH
    )
    f_right = jnp.einsum("kba,kbn->kan", couple, left, precision=HIGH) + jnp.einsum(
        "kab,kbn->kan", transfer[:, :, width:], parent, precision=HIGH
    )
    return jnp.stack([f_left, f_right], axis=1).reshape(-1, width, left.shape[2])


def pick_row(array, index):
    return lax.dynamic_index_in_dim(array, index, 0, keepdims=True)


def on_device(
    coords,
    perm,
    inv_scale,
    noise,
    leaf_basis,
    pair_transfer,
    coupling,
    solution,
    residual,
    direction,
):
    rows = perm.shape[0]
    nleaves = rows // LEAF
    local_heights = nleaves.bit_length() - 1
    devices = lax.axis_size(("group", "within"))
    upper_heights = devices.bit_length() - 1
    rank = leaf_basis.shape[1]
    columns = direction.shape[1]
    me_index = lax.axis_index(("group", "within"))
    points = (coords[perm] * inv_scale).reshape(nleaves, LEAF, coords.shape[1])
    vectors = direction.reshape(nleaves, LEAF, columns)
    basis = leaf_basis.reshape(nleaves, LEAF, rank)
    coeff = jnp.einsum("lpr,lpn->lrn", basis, vectors, precision=HIGH)
    stacked = []
    for height in range(1, local_heights + 1):
        chosen = pair_transfer[2 ** (height - 1) - 1 :: 2**height]
        left, right = (coeff[0::2], coeff[1::2])
        stacked.append((left, right))
        coeff = raise_pair(chosen, left, right)
    own_transfer = pair_transfer[nleaves - 1 :]
    own_couple = coupling[nleaves - 1 :]
    path = []
    all_coeff = lax.all_gather(coeff, ("group", "within"), axis=0, tiled=True)
    all_transfer, all_couple = (
        lax.all_gather(own_transfer, ("group", "within"), axis=0, tiled=True),
        lax.all_gather(own_couple, ("group", "within"), axis=0, tiled=True),
    )
    level_coeff = all_coeff
    for step in range(upper_heights):
        height = step + 1
        chosen = all_transfer[2 ** (height - 1) - 1 :: 2**height]
        couple = all_couple[2 ** (height - 1) - 1 :: 2**height]
        left, right = (level_coeff[0::2], level_coeff[1::2])
        node = me_index >> height
        is_left = me_index >> step & 1 == 0
        path.append(
            (
                is_left,
                pick_row(chosen, node),
                pick_row(couple, node),
                pick_row(left, node),
                pick_row(right, node),
            )
        )
        if step + 1 < upper_heights:
            level_coeff = raise_pair(chosen, left, right)
    far = jnp.zeros((1, rank, columns), jnp.float32)
    for is_left, node_transfer, node_couple, left, right in reversed(path):
        both = lower_pair(node_transfer, node_couple, left, right, far)
        far = jnp.where(is_left, both[0:1], both[1:2])
    for height in range(local_heights, 0, -1):
        chosen = pair_transfer[2 ** (height - 1) - 1 :: 2**height]
        couple = coupling[2 ** (height - 1) - 1 :: 2**height]
        left, right = stacked[height - 1]
        far = lower_pair(chosen, couple, left, right, far)
    dense = lax.map(leaf_product, (points, vectors))
    image = dense + noise[0] * vectors + jnp.einsum("lpr,lrn->lpn", basis, far, precision=HIGH)
    image = image.reshape(rows, columns)
    old_rr = lax.psum(jnp.sum(residual * residual, axis=0), ("group", "within"))
    curve = lax.psum(jnp.sum(direction * image, axis=0), ("group", "within"))
    alpha = old_rr / curve
    new_residual = residual - alpha * image
    new_rr = lax.psum(jnp.sum(new_residual * new_residual, axis=0), ("group", "within"))
    new_solution = solution + alpha * direction
    new_direction = new_residual + new_rr / old_rr * direction
    return (new_solution, new_residual, new_direction)


def solution(mesh):
    in_specs = (
        P(("group", "within"), None),
        P(("group", "within")),
        P(),
        P(),
        P(("group", "within"), None),
        P(("group", "within"), None, None),
        P(("group", "within"), None, None),
        P(("group", "within"), None),
        P(("group", "within"), None),
        P(("group", "within"), None),
    )
    out_specs = (
        P(("group", "within"), None),
        P(("group", "within"), None),
        P(("group", "within"), None),
    )
    return jax.shard_map(
        on_device, mesh=mesh, in_specs=in_specs, out_specs=out_specs, check_vma=False
    )
```

profile of v0, /device:TPU:1, one launch (start us, length us, event | category | flops | bytes accessed | tf_op | source)
XLA Modules:
  0.0 593.2 jit_solution(14687438414667947650)
XLA Ops:
  10.5 2.6 fusion.61
  23.7 14.2 %gather_fusion = f32[4096,64]{1,0:T(8,128)} fusion(f32[4096,64]{1,0:T(8,128)S(1)} %copy.41, s32[4096]{0:T(1024)S(1)} %fusion.196), kind=kCustom, calls=%fused_computation | custom fusion | bytes 2113536 | tf_op jit(solution)/shard_map/gather | solution.py:68
  47.6 3.1 broadcast_multiply_fusion
  50.7 56.3 %while.10 = (s32[]{:T(128)}, f32[8,512,64]{1,2,0:T(8,128)}, f32[8,512,64]{2,1,0:T(8,128)}, f32[8,512,64]{1,0,2:T(8,128)}, s32[]{:T(128)}) while((s32[]{:T(128)}, f32[8,512,64]{1,2,0:T(8,128)}, f32[8,512,64]{2,1,0:T(8,128)}, f32[8,512,64]{1,0,2:T(8,128)}, s32[]{:T(128)}) %tuple.44), condition=%wide.region_4.5_spmd, body=%wide.region_2.4_spmd.sunk | while | flops 405339648 | bytes 3284037 | solution.py:114
  51.8 2.1 fusion.281
  55.4 2.3 fusion.282
  58.8 2.2 fusion.281
  62.5 2.3 fusion.282
  69.5 2.3 fusion.282
  76.4 2.3 fusion.282
  79.8 2.2 fusion.281
  83.5 2.3 fusion.282
  90.4 2.3 fusion.282
  93.8 2.1 fusion.281
  97.4 2.3 fusion.282
  104.4 2.3 fusion.282
  107.1 27.1 %all-gather.5.cloned.1.call-done = f32[256,64,64]{2,1,0:T(8,128)} async-done(((f32[1,64,64]{2,1,0:T(8,128)}), f32[256,64,64]{2,1,0:T(8,128)}) %all-gather.5.cloned.1.call-update) | async-done | bytes 4194320 | tf_op jit(solution)/shard_map/all_gather | solution.py:84
  140.7 2.3 slice.325
  143.0 3.2 slice.318
  146.2 4.8 slice.310
  151.0 102.0 %all-gather.9.cloned.1.call-done = f32[16384,64]{1,0:T(8,128)} async-done(((f32[64,64]{1,0:T(8,128)}), f32[16384,64]{1,0:T(8,128)}) %all-gather.9.cloned.1.call-update) | async-done | bytes 4194320 | tf_op jit(solution)/shard_map/all_gather | solution.py:81
  253.0 4.3 fusion.245
  260.5 111.2 %all-gather.7.cloned.1.call-done = f32[256,64,128]{2,1,0:T(8,128)} async-done(((f32[1,64,128]{2,1,0:T(8,128)}), f32[256,64,128]{2,1,0:T(8,128)}) %all-gather.7.cloned.1.call-update) | async-done | bytes 8388624 | tf_op jit(solution)/shard_map/all_gather | solution.py:83
  371.7 2.9 slice.316
  376.4 7.8 %fusion.24 = f32[128,64,64]{2,1,0:T(8,128)S(1)} fusion(f32[128,64,128]{2,1,0:T(8,128)S(1)} %slice.316, f32[256,64,64]{2,1,0:T(8,128)S(1)} %bitcast.283), kind=kOutput, calls=%fused_computation.29 | convolution fusion | flops 402653184 | bytes 10485760 | tf_op jit(solution)/shard_map/kab,kan->kbn/dot_general | solution.py:30
  384.2 7.0 %add_bitcast_fusion = f32[128,64,64]{1,2,0:T(8,128)S(1)} fusion(f32[128,64,64]{2,1,0:T(8,128)S(1)} %fusion.24, f32[128,64,128]{2,1,0:T(8,128)S(1)} %slice.316, f32[256,64,64]{2,1,0:T(8,128)S(1)} %bitcast.284), kind=kOutput, calls=%fused_computation.33 | convolution fusion | flops 403177472 | bytes 14680064 | tf_op jit(solution)/shard_map/kab,kan->kbn/dot_general | solution.py:29
  393.5 2.4 fusion.30
  395.9 2.5 add_bitcast_fusion.1
  431.2 2.3 fusion.38
  433.9 74.5 %all-reduce = (f32[64]{0:T(128)S(1)}, f32[64]{0:T(128)S(1)}) all-reduce(f32[64]{0:T(128)S(1)} %get-tuple-element.67, f32[64]{0:T(128)S(1)} %get-tuple-element.66), channel_id=1, replica_groups=mesh['group'=4,'within'=64] {'group','within'}, use_global_device_ids=true, to_apply=%region_1.2 | all-reduce | flops 128 | bytes 1024 | tf_op jit(solution)/shard_map/psum | solution.py:117
  509.7 73.6 %psum.23 = f32[64]{0:T(128)S(1)} all-reduce(f32[64]{0:T(128)S(1)} %get-tuple-element.48), channel_id=1, replica_groups=mesh['group'=4,'within'=64] {'group','within'}, use_global_device_ids=true, to_apply=%region_8.9 | all-reduce | flops 64 | bytes 512 | tf_op jit(solution)/shard_map/psum | solution.py:121
  583.3 3.1 multiply_add_fusion
  (162 shorter events, 99.4 us)
Async XLA Ops:
  7.2 13.5 %copy-start.1 = (f32[4096,64]{0,1:T(8,128)S(1)}, f32[4096,64]{0,1:T(8,128)}, u32[]{:S(2)}) copy-start(f32[4096,64]{0,1:T(8,128)} %param.21) | copy-start | bytes 3145732
  7.2 127.0 %all-gather.5.cloned.1.call-start = ((), (), s32[]{:S(2)}) async-start(), calls=%async_computation | async-start | bytes 8421376 | tf_op jit(solution)/shard_map/all_gather | solution.py:84
  8.7 244.3 %all-gather.9.cloned.1.call-start = ((), (), s32[]{:S(2)}) async-start(), calls=%async_computation.2 | async-start | bytes 8421376 | tf_op jit(solution)/shard_map/all_gather | solution.py:81
  10.5 3.7 copy-start.4
  14.0 0.7 copy-start.6
  14.7 0.9 copy-start.7
  17.4 354.4 %all-gather.7.cloned.1.call-start = ((), (), s32[]{:S(2)}) async-start(), calls=%async_computation.1 | async-start | bytes 8421376 | tf_op jit(solution)/shard_map/all_gather | solution.py:83
  371.7 4.7 copy-start
  404.6 5.7 copy-start.10
  404.6 6.1 %copy-start.9 = (f32[4,64,64]{2,1,0:T(8,128)S(1)}, f32[4,64,64]{2,1,0:T(8,128)}, u32[]{:S(2)}) copy-start(f32[4,64,64]{2,1,0:T(8,128)} %slice.346) | copy-start | bytes 196612
  405.3 20.0 %copy-start.16 = (f32[64,64]{1,0:T(8,128)S(1)}, f32[64,64]{1,0:T(8,128)}, u32[]{:S(2)}) copy-start(f32[64,64]{1,0:T(8,128)} %fusion.113) | copy-start | bytes 49156
  405.4 20.2 %copy-start.13 = (f32[64,64]{1,0:T(8,128)S(1)}, f32[64,64]{1,0:T(8,128)}, u32[]{:S(2)}) copy-start(f32[64,64]{1,0:T(8,128)} %fusion.111) | copy-start | bytes 49156
  405.4 20.4 %copy-start.15 = (f32[64,64]{1,0:T(8,128)S(1)}, f32[64,64]{1,0:T(8,128)}, u32[]{:S(2)}) copy-start(f32[64,64]{1,0:T(8,128)} %fusion.160) | copy-start | bytes 49156
  406.4 20.4 %copy-start.14 = (f32[64,64]{1,0:T(8,128)S(1)}, f32[64,64]{1,0:T(8,128)}, u32[]{:S(2)}) copy-start(f32[64,64]{1,0:T(8,128)} %fusion.158) | copy-start | bytes 49156
  406.4 21.5 %copy-start.5 = (f32[2,64,128]{2,1,0:T(8,128)S(1)}, f32[2,64,128]{2,1,0:T(8,128)}, u32[]{:S(2)}) copy-start(f32[2,64,128]{2,1,0:T(8,128)} %copy-done.4) | copy-start | bytes 196612
  406.4 21.5 %copy-start.12 = (f32[2,64,64]{2,1,0:T(8,128)S(1)}, f32[2,64,64]{2,1,0:T(8,128)}, u32[]{:S(2)}) copy-start(f32[2,64,64]{2,1,0:T(8,128)} %fusion.105) | copy-start | bytes 98308
  406.4 21.7 %copy-start.11 = (f32[2,64,64]{2,1,0:T(8,128)S(1)}, f32[2,64,64]{2,1,0:T(8,128)}, u32[]{:S(2)}) copy-start(f32[2,64,64]{2,1,0:T(8,128)} %fusion.101) | copy-start | bytes 98308
  407.3 21.7 %copy-start.8 = (f32[4,64,64]{2,1,0:T(8,128)S(1)}, f32[4,64,64]{2,1,0:T(8,128)}, u32[]{:S(2)}) copy-start(f32[4,64,64]{2,1,0:T(8,128)} %fusion.85) | copy-start | bytes 196612
  408.5 22.7 %copy-start.2 = (f32[4096,64]{0,1:T(8,128)S(1)}, f32[4096,64]{0,1:T(8,128)}, u32[]{:S(2)}) copy-start(f32[4096,64]{0,1:T(8,128)} %param.16) | copy-start | bytes 3145732
  429.0 4.7 copy-start.3
Sparse Core Ops, SparseCore 0:
  11.7 122.3 all-gather.4
  137.9 115.0 all-gather.8
  256.7 114.9 all-gather.6
where the time goes:
time: 602 us; the launch traced here: 593 us
  waiting for transfers between devices  240 us (40%)
  blocking collectives  148 us (25%)
  matrix products  101 us (17%)
  local copies, waits for them, and re-layouts  70 us (12%)
  other arithmetic  18 us (3%)
  between operations  15.5 us (3%)
    all_gather x1, waiting for transfers between devices, on_device(): lax.all_gather(own_transfer, ('group', 'within'), axis=0, tiled=True)  111 us
    all_gather x1, waiting for transfers between devices, on_device(): all_coeff = lax.all_gather(coeff, ('group', 'within'), axis=0, tiled=True)  102 us
    psum x1, blocking collectives, on_device(): old_rr = lax.psum(jnp.sum(residual * residual, axis=0), ('group', 'within'))  74.5 us
    psum x1, blocking collectives, on_device(): lax.psum(jnp.sum(new_residual * new_residual, axis=0), ('group', 'within'))  73.6 us
    all_gather x1, waiting for transfers between devices, on_device(): lax.all_gather(own_couple, ('group', 'within'), axis=0, tiled=True)  27.1 us
    dot_general x8, matrix products, leaf_product(): return jnp.dot(matern_block(item[0]), item[1], precision=HIGH)  18.1 us
    dot_general x8, matrix products, matern_block(): inner = jnp.dot(scaled, scaled.T, precision=HIGH)  17 us
    slice x7, local copies, waits for them, and re-layouts, on_device(): couple = all_couple[2 ** (height - 1) - 1::2 ** height]  16.9 us
  transfers between devices with their start and end apart: 3, of which 3 were waited for; matrix products, arithmetic and copies ran while one was open for 20% of the time, Pallas kernels for 0%

commit v1 on v0

v1 whole, which is shorter than its diff:
```python
import functools
import math

import jax
import jax.numpy as jnp
from jax import lax
from jax.experimental import pallas as pl
from jax.experimental.pallas import tpu as pltpu
from jax.sharding import PartitionSpec as P

LEAF = 512
RANK = 64
COLS = 64
ROWS = 4096
NLEAF = 8
ROOT_FIVE = math.sqrt(5.0)
MESH = pl.DeviceIdType.MESH
F32 = jnp.float32
BF16 = jnp.bfloat16
NT = (((1,), (1,)), ((), ()))
NN = (((1,), (0,)), ((), ()))


def split(a):
    high = a.astype(BF16)
    return high, (a - high.astype(F32)).astype(BF16)


def mxu(a, b, dims=NN):
    return lax.dot_general(a, b, dims, preferred_element_type=F32)


def product(a, b, dims=NN):
    ah, al = split(a)
    bh, bl = split(b)
    return mxu(ah, bh, dims) + (mxu(ah, bl, dims) + mxu(al, bh, dims))


def pack(c):
    return jnp.concatenate([c[0:32], c[32:64]], axis=1)


def unpack(p):
    return jnp.concatenate([p[:, 0:64], p[:, 64:128]], axis=0)


def raise_pair(transfer, left, right):
    return product(
        jnp.concatenate([left, right], axis=1),
        jnp.concatenate([transfer[:, 0:64], transfer[:, 64:128]], axis=0),
    )


def lower_left(transfer, couple, right, parent):
    return product(
        jnp.concatenate([right, parent], axis=1),
        jnp.concatenate([couple, transfer[:, 0:64]], axis=1),
        NT,
    )


def lower_right(transfer, couple, left, parent):
    return product(
        jnp.concatenate([left, parent], axis=1),
        jnp.concatenate([couple.T, transfer[:, 64:128]], axis=1),
        NT,
    )


def lower_side(is_left, transfer, couple, sibling, parent):
    side = jnp.where(is_left, transfer[:, 0:64], transfer[:, 64:128])
    across = jnp.where(is_left, couple, couple.T)
    if parent is None:
        return product(sibling, across, NT)
    return product(
        jnp.concatenate([sibling, parent], axis=1),
        jnp.concatenate([across, side], axis=1),
        NT,
    )


def kernel(
    coords, perm, scale, noise, basis, transfer, coupling, sol, res, direc,
    out_sol, out_res, out_dir,
    x_in, x_rows, x_perm, b_in, t_in, k_in, s_in, r_in, d_in, image,
    d_split, b_split, leaf_c, leaf_f,
    mat_a, mat_z, mat_x, c_a, c_z, c_x, f_top, pair_c, reduce,
    in_sem, out_sem, send_sem, rm_a, rm_z, rm_x, rc_a, rc_z, rc_x, r_f, r_red,
):
    group = lax.axis_index("group")
    within = lax.axis_index("within")
    slab = group
    line = lax.div(within, 8)
    spot = lax.rem(within, 8)
    leader = spot == 7
    top_line = line == 7

    def in_plane(q):
        return (group, line * 8 + q)

    def in_line(q):
        return (group, q * 8 + spot)

    def in_slab(q):
        return (q, within)

    inputs = [
        (transfer, t_in), (coupling, k_in), (direc, d_in), (basis, b_in),
        (coords, x_in), (res, r_in), (sol, s_in),
    ]
    loads = [
        pltpu.make_async_copy(src, dst, in_sem.at[i]) for i, (src, dst) in enumerate(inputs)
    ]
    for load in loads:
        load.start()

    barrier = pltpu.get_barrier_semaphore()

    def greet(device):
        pl.semaphore_signal(barrier, inc=1, device_id=device, device_id_type=MESH)

    for p in range(1, 8):
        greet(in_plane(lax.rem(spot + p, 8)))
        greet(in_line(lax.rem(line + p, 8)))
    for p in range(1, 4):
        greet(in_slab(lax.rem(slab + p, 4)))

    @pl.when(jnp.logical_and(leader, jnp.logical_not(top_line)))
    def _():
        for q in range(3):
            @pl.when(slab != q)
            def _():
                greet((q, 63))

    sends = []

    def remote(src, dst, recv, device):
        index = len(sends)
        copy = pltpu.make_async_remote_copy(
            src_ref=src, dst_ref=dst, send_sem=send_sem.at[index], recv_sem=recv,
            device_id=device, device_id_type=MESH,
        )
        sends.append(copy)
        return copy

    def arrived(dst, recv):
        pltpu.make_async_remote_copy(
            src_ref=dst, dst_ref=dst, send_sem=send_sem.at[0], recv_sem=recv,
            device_id=in_plane(lax.rem(spot + 1, 8)), device_id_type=MESH,
        ).wait_recv()

    loads[0].wait()
    loads[1].wait()
    own = jnp.concatenate([t_in[7], pack(k_in[7])], axis=0)

    @pl.when(jnp.logical_not(leader))
    def _():
        mat_a[spot] = own

    @pl.when(jnp.logical_and(leader, jnp.logical_not(top_line)))
    def _():
        mat_z[line] = own

    @pl.when(jnp.logical_and(leader, top_line))
    def _():
        mat_x[slab] = own

    owner = jnp.logical_and(jnp.logical_and(leader, top_line), slab < 3)
    pl.semaphore_wait(barrier, jnp.where(owner, 38, 17))

    send_a = [
        remote(mat_a.at[spot], mat_a.at[spot], rm_a.at[spot], in_plane(lax.rem(spot + p, 8)))
        for p in range(1, 8)
    ]
    send_z = [
        remote(mat_z.at[line], mat_z.at[line], rm_z.at[line], in_line(lax.rem(line + p, 8)))
        for p in range(1, 8)
    ]
    first_x = len(sends)
    flat = slab * 8 + line

    def send_top(p):
        q = lax.rem(flat + p, 32)
        return pltpu.make_async_remote_copy(
            src_ref=mat_x.at[slab], dst_ref=mat_x.at[slab], send_sem=send_sem.at[first_x + p - 1],
            recv_sem=rm_x.at[slab], device_id=(lax.div(q, 8), lax.rem(q, 8) * 8 + 7), device_id_type=MESH,
        )
    sends.extend([None] * 31)

    @pl.when(jnp.logical_not(leader))
    def _():
        for copy in send_a:
            copy.start()

    @pl.when(jnp.logical_and(leader, jnp.logical_not(top_line)))
    def _():
        for copy in send_z:
            copy.start()

    @pl.when(owner)
    def _():
        @pl.loop(1, 32)
        def _(p):
            send_top(p).start()

    loads[2].wait()
    loads[3].wait()

    @pl.loop(0, NLEAF)
    def _(leaf):
        at = pl.multiple_of(leaf * LEAF, LEAF)
        dh, dl = split(d_in[:, pl.ds(at, LEAF)])
        bh, bl = split(b_in[:, pl.ds(at, LEAF)])
        both_d = jnp.concatenate([dh, dl], axis=0)
        both_b = jnp.concatenate([bh, bl], axis=0)
        d_split[:, pl.ds(at, LEAF)] = both_d
        b_split[:, pl.ds(at, LEAF)] = both_b
        prod = mxu(both_d, both_b, NT)
        leaf_c[leaf] = (prod[0:64, 0:64] + prod[64:128, 64:128]) + (prod[0:64, 64:128] + prod[64:128, 0:64])

    for k in range(4):
        leaf_c[8 + k] = raise_pair(t_in[2 * k], leaf_c[2 * k], leaf_c[2 * k + 1])
    for k in range(2):
        leaf_c[12 + k] = raise_pair(t_in[4 * k + 1], leaf_c[8 + 2 * k], leaf_c[9 + 2 * k])
    c_a[spot] = pack(raise_pair(t_in[3], leaf_c[12], leaf_c[13]))
    send_ca = [
        remote(c_a.at[spot], c_a.at[spot], rc_a.at[spot], in_plane(lax.rem(spot + p, 8)))
        for p in range(1, 8)
    ]
    for copy in send_ca:
        copy.start()

    loads[4].wait()

    @pl.loop(0, ROWS // 128)
    def _(i):
        at = pl.multiple_of(i * 128, 128)
        x_rows[pl.ds(at, 128), 0:64] = x_in[:, pl.ds(at, 128)].T * (ROOT_FIVE * scale[...])

    def dense(first, last):
        @pl.loop(first, last)
        def _(leaf):
            at = pl.multiple_of(leaf * LEAF, LEAF)

            @pl.loop(0, LEAF // 32)
            def _(i):
                base = pl.multiple_of(i * 32, 32)
                for j in range(32):
                    x_perm[pl.ds(base + j, 1), :] = x_rows[pl.ds(perm[at + base + j], 1), :]

            xh, xl = split(x_perm[:, 0:64])
            near = xh.astype(F32) + xl.astype(F32)
            square = jnp.sum(near * near, axis=1, keepdims=True)
            square_row = jnp.broadcast_to(square, (LEAF, 128)).T[0:1]
            one = jnp.concatenate([xh, xh, xl, xl], axis=1)
            two = jnp.concatenate([xh, xl, xh, xl], axis=1)
            vectors = d_split[:, pl.ds(at, LEAF)].T
            for c in range(0, LEAF, 128):
                inner = mxu(one[c : c + 128], two, NT)
                dist_sq = jnp.maximum((square[c : c + 128] + square_row) - 2.0 * inner, 1e-30)
                dist = dist_sq * lax.rsqrt(dist_sq)
                value = (1.0 + dist + dist_sq * (1.0 / 3.0)) * jnp.exp(-dist)
                vh, vl = split(value)
                got = mxu(vh, vectors) + mxu(vl, vectors)
                image[:, pl.ds(at + c, 128)] = (got[:, 0:64] + got[:, 64:128]).T

    def mats(ref):
        return ref[0:64, :], unpack(ref[64:96, :])

    dense(0, 3)

    for p in range(1, 8):
        q = lax.rem(spot + p, 8)
        arrived(c_a.at[q], rc_a.at[q])

        @pl.when(q != 7)
        def _():
            arrived(mat_a.at[q], rm_a.at[q])
    for k in range(4):
        pair_c[k] = raise_pair(mat_a[2 * k, 0:64, :], unpack(c_a[2 * k]), unpack(c_a[2 * k + 1]))
    for k in range(2):
        pair_c[4 + k] = raise_pair(mat_a[4 * k + 1, 0:64, :], pair_c[2 * k], pair_c[2 * k + 1])

    send_cz = [
        remote(c_z.at[line], c_z.at[line], rc_z.at[line], in_line(lax.rem(line + p, 8)))
        for p in range(1, 8)
    ]
    send_cx = [
        remote(c_x.at[slab], c_x.at[slab], rc_x.at[slab], in_slab(lax.rem(slab + p, 4)))
        for p in range(1, 4)
    ]
    send_f = [
        remote(f_top, f_top, r_f, in_plane(lax.rem(spot + p, 8)))
        for p in range(1, 8)
    ]

    @pl.when(leader)
    def _():
        c_z[line] = pack(raise_pair(mat_a[3, 0:64, :], pair_c[4], pair_c[5]))
        for copy in send_cz:
            copy.start()

    dense(3, 5)

    @pl.when(leader)
    def _():
        for p in range(1, 8):
            q = lax.rem(line + p, 8)
            arrived(c_z.at[q], rc_z.at[q])

            @pl.when(q != 7)
            def _():
                arrived(mat_z.at[q], rm_z.at[q])
        for k in range(4):
            pair_c[6 + k] = raise_pair(mat_z[2 * k, 0:64, :], unpack(c_z[2 * k]), unpack(c_z[2 * k + 1]))
        for k in range(2):
            pair_c[10 + k] = raise_pair(mat_z[4 * k + 1, 0:64, :], pair_c[6 + 2 * k], pair_c[7 + 2 * k])
        c_x[slab] = pack(raise_pair(mat_z[3, 0:64, :], pair_c[10], pair_c[11]))
        for copy in send_cx:
            copy.start()

    dense(5, 7)

    @pl.when(leader)
    def _():
        for p in range(1, 4):
            q = lax.rem(slab + p, 4)
            arrived(c_x.at[q], rc_x.at[q])
        for q in range(3):
            @pl.when(jnp.logical_or(slab != q, jnp.logical_not(top_line)))
            def _():
                arrived(mat_x.at[q], rm_x.at[q])
        for k in range(2):
            pair_c[12 + k] = raise_pair(mat_x[2 * k, 0:64, :], unpack(c_x[2 * k]), unpack(c_x[2 * k + 1]))
        half = lax.div(slab, 2)
        t, b = mats(mat_x.at[1])
        far = lower_side(half == 0, t, b, pair_c[13 - half], None)
        t, b = mats(mat_x.at[half * 2])
        side = lax.rem(slab, 2)
        far = lower_side(side == 0, t, b, unpack(c_x[half * 2 + 1 - side]), far)
        half = lax.div(line, 4)
        t, b = mats(mat_z.at[3])
        far = lower_side(half == 0, t, b, pair_c[11 - half], far)
        quarter = lax.div(line, 2)
        side = lax.rem(quarter, 2)
        t, b = mats(mat_z.at[half * 4 + 1])
        far = lower_side(side == 0, t, b, pair_c[6 + half * 2 + 1 - side], far)
        side = lax.rem(line, 2)
        t, b = mats(mat_z.at[quarter * 2])
        far = lower_side(side == 0, t, b, unpack(c_z[quarter * 2 + 1 - side]), far)
        f_top[...] = pack(far)
        for copy in send_f:
            copy.start()

    dense(7, 8)

    @pl.when(jnp.logical_not(leader))
    def _():
        arrived(f_top, r_f)
    far = unpack(f_top[...])
    half = lax.div(spot, 4)
    t, b = mats(mat_a.at[3])
    far = lower_side(half == 0, t, b, pair_c[5 - half], far)
    quarter = lax.div(spot, 2)
    side = lax.rem(quarter, 2)
    t, b = mats(mat_a.at[half * 4 + 1])
    far = lower_side(side == 0, t, b, pair_c[half * 2 + 1 - side], far)
    side = lax.rem(spot, 2)
    t, b = mats(mat_a.at[quarter * 2])
    far = lower_side(side == 0, t, b, unpack(c_a[quarter * 2 + 1 - side]), far)
    near = [far]
    for height, first in ((3, 12), (2, 8), (1, 0)):
        below = []
        for k, parent in enumerate(near):
            node = k * 2**height + 2 ** (height - 1) - 1
            left, right = leaf_c[first + 2 * k], leaf_c[first + 2 * k + 1]
            below.append(lower_left(t_in[node], k_in[node], right, parent))
            below.append(lower_right(t_in[node], k_in[node], left, parent))
        near = below
    for k in range(NLEAF):
        fh, fl = split(near[k])
        leaf_f[k] = jnp.concatenate(
            [jnp.concatenate([fh, fh], axis=1), jnp.concatenate([fl, fl], axis=1)], axis=0
        )

    loads[5].wait()
    loads[6].wait()
    shift = noise[0]
    zero = jnp.zeros((COLS, 128), F32)

    def add_leaf(leaf, sums):
        at = pl.multiple_of(leaf * LEAF, LEAF)
        far = mxu(leaf_f[leaf], b_split[:, pl.ds(at, LEAF)])
        d = d_in[:, pl.ds(at, LEAF)]
        r = r_in[:, pl.ds(at, LEAF)]
        q = image[:, pl.ds(at, LEAF)] + shift * d + (far[0:64] + far[64:128])
        image[:, pl.ds(at, LEAF)] = q
        terms = (r * r, d * q, r * q, q * q)
        return tuple(
            total + ((term[:, 0:128] + term[:, 128:256]) + (term[:, 256:384] + term[:, 384:512]))
            for total, term in zip(sums, terms)
        )

    sums = lax.fori_loop(0, NLEAF, add_leaf, (zero, zero, zero, zero))
    lane = lax.broadcasted_iota(jnp.int32, (COLS, 128), 1)
    table = zero
    for i, total in enumerate(sums):
        table = jnp.where(lane == i, jnp.sum(total, axis=1, keepdims=True), table)
    value = table.T[0:8, :]

    first = 0
    send_red = []
    for size, place, device in ((8, spot, in_plane), (8, line, in_line), (4, slab, in_slab)):
        reduce[first + place, :, 0:64] = value
        copies = []
        for p in range(1, size):
            q = lax.rem(place + p, size)
            copies.append(
                remote(reduce.at[first + place], reduce.at[first + place], r_red.at[first + place], device(q))
            )
        for copy in copies:
            copy.start()
        send_red.extend(copies)
        for p in range(1, size):
            q = lax.rem(place + p, size)
            arrived(reduce.at[first + q], r_red.at[first + q])
        value = reduce[first, :, 0:64]
        for q in range(1, size):
            value = value + reduce[first + q, :, 0:64]
        first += size

    old, curve, cross, own_square = value[0:1], value[1:2], value[2:3], value[3:4]
    alpha = old / curve
    new = old - 2.0 * alpha * cross + alpha * alpha * own_square
    ratio = new / old
    alpha = jnp.broadcast_to(alpha, (128, COLS)).T
    ratio = jnp.broadcast_to(ratio, (128, COLS)).T
    alpha = jnp.concatenate([alpha] * 4, axis=1)
    ratio = jnp.concatenate([ratio] * 4, axis=1)

    def stores(leaf):
        at = pl.multiple_of(leaf * LEAF, LEAF)
        return [
            pltpu.make_async_copy(src.at[:, pl.ds(at, LEAF)], dst.at[:, pl.ds(at, LEAF)], out_sem.at[i, leaf])
            for i, (src, dst) in enumerate(((s_in, out_sol), (r_in, out_res), (image, out_dir)))
        ]

    @pl.loop(0, NLEAF)
    def _(leaf):
        at = pl.multiple_of(leaf * LEAF, LEAF)
        d = d_in[:, pl.ds(at, LEAF)]
        r = r_in[:, pl.ds(at, LEAF)] - alpha * image[:, pl.ds(at, LEAF)]
        s_in[:, pl.ds(at, LEAF)] = s_in[:, pl.ds(at, LEAF)] + alpha * d
        r_in[:, pl.ds(at, LEAF)] = r
        image[:, pl.ds(at, LEAF)] = r + ratio * d
        for copy in stores(leaf):
            copy.start()

    for copy in send_ca + send_red:
        copy.wait_send()

    @pl.when(jnp.logical_not(leader))
    def _():
        for copy in send_a:
            copy.wait_send()

    @pl.when(leader)
    def _():
        for copy in send_cz + send_cx + send_f:
            copy.wait_send()

    @pl.when(jnp.logical_and(leader, jnp.logical_not(top_line)))
    def _():
        for copy in send_z:
            copy.wait_send()

    @pl.when(owner)
    def _():
        @pl.loop(1, 32)
        def _(p):
            send_top(p).wait_send()

    @pl.loop(0, NLEAF)
    def _(leaf):
        for copy in stores(leaf):
            copy.wait()


def on_device(
    coords, perm, inv_scale, noise, leaf_basis, pair_transfer, coupling, solution, residual, direction
):
    hbm = pl.BlockSpec(memory_space=pl.ANY)
    smem = pl.BlockSpec(memory_space=pltpu.SMEM)
    vmem = pl.BlockSpec(memory_space=pltpu.VMEM)
    wide = jax.ShapeDtypeStruct((COLS, ROWS), F32)
    dma = pltpu.SemaphoreType.DMA
    outs = pl.pallas_call(
        kernel,
        out_shape=(wide, wide, wide),
        in_specs=[hbm, smem, vmem, smem, hbm, hbm, hbm, hbm, hbm, hbm],
        out_specs=(hbm, hbm, hbm),
        scratch_shapes=[
            pltpu.VMEM((64, ROWS), F32),
            pltpu.VMEM((ROWS, 128), F32),
            pltpu.VMEM((LEAF, 128), F32),
            pltpu.VMEM((64, ROWS), F32),
            pltpu.VMEM((8, 64, 128), F32),
            pltpu.VMEM((8, 64, 64), F32),
            pltpu.VMEM((64, ROWS), F32),
            pltpu.VMEM((64, ROWS), F32),
            pltpu.VMEM((64, ROWS), F32),
            pltpu.VMEM((64, ROWS), F32),
            pltpu.VMEM((128, ROWS), BF16),
            pltpu.VMEM((128, ROWS), BF16),
            pltpu.VMEM((14, 64, 64), F32),
            pltpu.VMEM((8, 128, 128), BF16),
            pltpu.VMEM((8, 96, 128), F32),
            pltpu.VMEM((8, 96, 128), F32),
            pltpu.VMEM((4, 96, 128), F32),
            pltpu.VMEM((8, 32, 128), F32),
            pltpu.VMEM((8, 32, 128), F32),
            pltpu.VMEM((4, 32, 128), F32),
            pltpu.VMEM((32, 128), F32),
            pltpu.VMEM((14, 64, 64), F32),
            pltpu.VMEM((20, 8, 128), F32),
            dma((7,)),
            dma((3, NLEAF)),
            dma((96,)),
            dma((8,)),
            dma((8,)),
            dma((4,)),
            dma((8,)),
            dma((8,)),
            dma((4,)),
            dma,
            dma((20,)),
        ],
        compiler_params=pltpu.CompilerParams(
            collective_id=0, has_side_effects=True, vmem_limit_bytes=50 * 2**20
        ),
        cost_estimate=pl.CostEstimate(flops=4 * 10**9, bytes_accessed=10 * 2**20, transcendentals=4 * 2**20),
        name="cg_step",
    )(
        coords.T, perm, inv_scale.reshape(1, 64), noise, leaf_basis.T, pair_transfer, coupling,
        solution.T, residual.T, direction.T,
    )
    return tuple(out.T for out in outs)


def solution(mesh):
    rows = P(("group", "within"), None)
    cubes = P(("group", "within"), None, None)
    in_specs = (rows, P(("group", "within")), P(), P(), rows, cubes, cubes, rows, rows, rows)
    return jax.shard_map(
        on_device, mesh=mesh, in_specs=in_specs, out_specs=(rows, rows, rows), check_vma=False
    )
```

time: 602 us -> 61.2 us (0.10); the launches traced: 593 us -> 61 us
  waiting for transfers between devices: 240 us -> 0 us
  blocking collectives: 148 us -> 0 us
  matrix products: 101 us -> 0 us
  local copies, waits for them, and re-layouts: 70 us -> 6.18 us
  Pallas kernels: 0 us -> 53.5 us
  other arithmetic: 18 us -> 0 us
  between operations: 15.5 us -> 1.3 us
    all_gather x3 -> x0, waiting for transfers between devices: 240 us -> none  [the longest x1 111 us: on_device(): lax.all_gather(own_transfer, ('group', 'within'), axis=0, tiled=True)]
    psum x2 -> x0, blocking collectives: 148 us -> none  [the longest x1 74.5 us: on_device(): old_rr = lax.psum(jnp.sum(residual * residual, axis=0), ('group', 'within'))]
    dot_general x82 -> x0, matrix products: 101 us -> none  [the longest x8 18.1 us: leaf_product(): return jnp.dot(matern_block(item[0]), item[1], precision=HIGH)]
    pallas_call x0 -> x1, Pallas kernels: none -> 53.5 us  [on_device(): pl.pallas_call(kernel, out_shape=(wide, wide, wide), in_specs=[hbm, smem,...]
    slice x24 -> x0, local copies, waits for them, and re-layouts: 32.4 us -> none  [the longest x7 16.9 us: on_device(): couple = all_couple[2 ** (height - 1) - 1::2 ** height]]
    gather x1 -> x0, local copies, waits for them, and re-layouts: 14.2 us -> none  [on_device(): points = (coords[perm] * inv_scale).reshape(nleaves, LEAF, coords.shape[1])]
    dynamic_slice x16 -> x0, local copies, waits for them, and re-layouts: 11.8 us -> none  [on_device(): dense = lax.map(leaf_product, (points, vectors))]
    reduce_sum x10 -> x0, other arithmetic: 10.3 us -> none  [the longest x8 8.75 us: matern_block(): squares = jnp.sum(scaled * scaled, axis=1)]
  transfers between devices with their start and end apart: 3 -> 0, of which waited for: 3 -> 0; matrix products, arithmetic and copies ran while one was open for 20% -> 0% of each run, Pallas kernels for 0% -> 0%
where the time goes in v1:
time: 61.2 us; the launch traced here: 61 us
  Pallas kernels  53.5 us (87%)
  local copies, waits for them, and re-layouts  6.18 us (10%)
  between operations  1.3 us (2%)
    pallas_call x1, Pallas kernels, on_device(): pl.pallas_call(kernel, out_shape=(wide, wide, wide), in_specs=[hbm, smem,...  53.5 us
    unnamed x11, local copies, waits for them, and re-layouts  6.18 us

profile of v1, /device:TPU:1, one launch (start us, length us, event | category | flops | bytes accessed | tf_op | source)
XLA Modules:
  0.0 61.0 jit_solution(7453965581095185924)
XLA Ops:
  1.3 0.0 copy-start.3
  1.3 0.6 %copy-done.3 = f32[64]{0:T(128)S(1)} copy-done((f32[64]{0:T(128)S(1)}, f32[64]{0:T(128)}, u32[]{:S(2)}) %copy-start.3) | copy-done | bytes 280
  1.9 0.0 copy-start
  1.9 0.9 %copy-done = f32[8,64,128]{2,1,0:T(8,128)S(1)} copy-done((f32[8,64,128]{2,1,0:T(8,128)S(1)}, f32[8,64,128]{2,1,0:T(8,128)}, u32[]{:S(2)}) %copy-start) | copy-done | bytes 262168
  2.9 0.0 copy-start.1
  2.9 0.9 %copy-done.1 = f32[8,64,64]{2,1,0:T(8,128)S(1)} copy-done((f32[8,64,64]{2,1,0:T(8,128)S(1)}, f32[8,64,64]{2,1,0:T(8,128)}, u32[]{:S(2)}) %copy-start.1) | copy-done | bytes 131096
  3.8 0.0 copy-start.2
  3.8 0.7 %copy-done.2 = s32[4096]{0:T(1024)S(1)} copy-done((s32[4096]{0:T(1024)S(1)}, s32[4096]{0:T(1024)}, u32[]{:S(2)}) %copy-start.2) | copy-done | bytes 16408
  4.6 53.5 %cg_step.1 = (f32[64,4096]{1,0:T(8,128)S(1)}, f32[64,4096]{1,0:T(8,128)S(1)}, f32[64,4096]{1,0:T(8,128)S(1)}) custom-call(f32[64,4096]{1,0:T(8,128)} %bitcast.13, s32[4096]{0:T(1024)S(1)} %copy-done.2, f32[1,64]{1,0:T(1,128)S(1)} %bitcast.12, f32[1]{0:T(128)S(6)} %copy.16.noise, f32[64,4096]{1,0:T(8,128)} %bitcast.14, f32[8,64,128]{2,1,0:T(8,128)S(1)} %copy-done, ...), custom_call_target="tpu_custom_call" | custom-call | flops 4000000000 | bytes 10485760 | tf_op jit(solution)/shard_map/cg_step/pallas_call | solution.py:497
  58.1 1.0 %copy.17 = f32[4096,64]{0,1:T(8,128)} copy(f32[4096,64]{0,1:T(8,128)S(1)} %bitcast.11) | data formatting | bytes 2097152
  59.1 1.0 %copy.18 = f32[4096,64]{0,1:T(8,128)} copy(f32[4096,64]{0,1:T(8,128)S(1)} %bitcast.10) | data formatting | bytes 2097152
  60.0 1.0 %copy.19 = f32[4096,64]{0,1:T(8,128)} copy(f32[4096,64]{0,1:T(8,128)S(1)} %bitcast.9) | data formatting | bytes 2097152
Async XLA Ops:
  1.3 0.7 %copy-start.3 = (f32[64]{0:T(128)S(1)}, f32[64]{0:T(128)}, u32[]{:S(2)}) copy-start(f32[64]{0:T(128)} %param.12) | copy-start | bytes 772
  1.9 0.9 %copy-start = (f32[8,64,128]{2,1,0:T(8,128)S(1)}, f32[8,64,128]{2,1,0:T(8,128)}, u32[]{:S(2)}) copy-start(f32[8,64,128]{2,1,0:T(8,128)} %transfer.1) | copy-start | bytes 786436
  2.9 0.9 %copy-start.1 = (f32[8,64,64]{2,1,0:T(8,128)S(1)}, f32[8,64,64]{2,1,0:T(8,128)}, u32[]{:S(2)}) copy-start(f32[8,64,64]{2,1,0:T(8,128)} %coupling.1) | copy-start | bytes 393220
  3.8 0.7 %copy-start.2 = (s32[4096]{0:T(1024)S(1)}, s32[4096]{0:T(1024)}, u32[]{:S(2)}) copy-start(s32[4096]{0:T(1024)} %perm.1) | copy-start | bytes 49156

commit v2 on v1

v2 whole, which is shorter than its diff:
```python
import functools
import math

import jax
import jax.numpy as jnp
from jax import lax
from jax.experimental import pallas as pl
from jax.experimental.pallas import tpu as pltpu
from jax.sharding import PartitionSpec as P

LEAF = 512
RANK = 64
COLS = 64
ROWS = 4096
NLEAF = 8
ROOT_FIVE = math.sqrt(5.0)
LN_TWO = math.log(2.0)
MESH = pl.DeviceIdType.MESH
FAR = (4, 3, 5, 2, 6, 1, 7)
F32 = jnp.float32
BF16 = jnp.bfloat16
NT = (((1,), (1,)), ((), ()))
NN = (((1,), (0,)), ((), ()))


def split(a):
    high = a.astype(BF16)
    return high, (a - high.astype(F32)).astype(BF16)


def mxu(a, b, dims=NN):
    return lax.dot_general(a, b, dims, preferred_element_type=F32)


def product(a, b, dims=NN):
    ah, al = split(a)
    bh, bl = split(b)
    return mxu(ah, bh, dims) + (mxu(ah, bl, dims) + mxu(al, bh, dims))


def pack(c):
    half = c.shape[0] // 2
    return jnp.concatenate([c[0:half], c[half:]], axis=1)


def unpack(p):
    return jnp.concatenate([p[:, 0:64], p[:, 64:128]], axis=0)


def raise_pair(transfer, left, right):
    return product(
        jnp.concatenate([left, right], axis=1),
        jnp.concatenate([transfer[:, 0:64], transfer[:, 64:128]], axis=0),
    )


def lower(left, transfer, couple, sibling, state):
    if isinstance(left, bool):
        side = transfer[:, 0:64] if left else transfer[:, 64:128]
        across = couple if left else couple.T
    else:
        side = jnp.where(left, transfer[:, 0:64], transfer[:, 64:128])
        across = jnp.where(left, couple, couple.T)
    none = jnp.zeros((64, 64), F32)
    return product(
        jnp.concatenate([jnp.concatenate([sibling, none], axis=0), state], axis=1),
        jnp.concatenate([across, side], axis=1),
        NT,
    )


def identity():
    row = lax.broadcasted_iota(jnp.int32, (128, 64), 0)
    column = lax.broadcasted_iota(jnp.int32, (128, 64), 1)
    return jnp.where(row == column + 64, 1.0, 0.0)


def lower_tree(mats, coefs):
    near = [identity()]
    for height, first in ((3, 12), (2, 8), (1, 0)):
        below = []
        for k, state in enumerate(near):
            t, b = mats(k * 2**height + 2 ** (height - 1) - 1)
            below.append(lower(True, t, b, coefs(first + 2 * k + 1), state))
            below.append(lower(False, t, b, coefs(first + 2 * k), state))
        near = below
    return jnp.concatenate(near, axis=1)


def kernel(
    coords, order, scale, noise, basis, transfer, coupling, res, direc,
    out_image, out_coef,
    perm, x_in, x_rows, x_perm, b_in, t_in, k_in, r_in, d_in, image,
    d_split, b_split, leaf_c, leaf_f,
    mat_a, mat_z, mat_x, paths, c_a, c_z, c_x, f_top, f_out, pair_c, reduce,
    local_f, local_op, plane_f, plane_op, slab_op,
    in_sem, out_sem, send_sem, rm_a, rm_z, rm_x, r_path, rc_a, rc_z, rc_x, r_f, r_red,
):
    group = lax.axis_index("group")
    within = lax.axis_index("within")
    slab = group
    line = lax.div(within, 8)
    spot = lax.rem(within, 8)
    leader = spot == 7
    top_line = line == 7

    def in_plane(q):
        return (group, line * 8 + q)

    def in_line(q):
        return (group, q * 8 + spot)

    def in_slab(q):
        return (q, within)

    inputs = [
        (transfer, t_in), (coupling, k_in), (direc, d_in), (basis, b_in),
        (coords, x_in), (order, perm), (res, r_in),
    ]
    loads = [
        pltpu.make_async_copy(src, dst, in_sem.at[i]) for i, (src, dst) in enumerate(inputs)
    ]
    for load in loads:
        load.start()

    barrier = pltpu.get_barrier_semaphore()

    def greet(device):
        pl.semaphore_signal(barrier, inc=1, device_id=device, device_id_type=MESH)

    for p in range(1, 8):
        greet(in_plane(lax.rem(spot + p, 8)))
        greet(in_line(lax.rem(line + p, 8)))
    for p in range(1, 4):
        greet(in_slab(lax.rem(slab + p, 4)))

    sends = []

    def remote(src, dst, recv, device):
        index = len(sends)
        copy = pltpu.make_async_remote_copy(
            src_ref=src, dst_ref=dst, send_sem=send_sem.at[index], recv_sem=recv,
            device_id=device, device_id_type=MESH,
        )
        sends.append(copy)
        return copy

    def arrived(dst, recv):
        pltpu.make_async_remote_copy(
            src_ref=dst, dst_ref=dst, send_sem=send_sem.at[0], recv_sem=recv,
            device_id=in_plane(lax.rem(spot + 1, 8)), device_id_type=MESH,
        ).wait_recv()

    loads[0].wait()
    loads[1].wait()
    own = jnp.concatenate([t_in[7], pack(k_in[7])], axis=0)

    @pl.when(jnp.logical_not(leader))
    def _():
        mat_a[spot] = own

    @pl.when(jnp.logical_and(leader, jnp.logical_not(top_line)))
    def _():
        mat_z[line] = own

    @pl.when(jnp.logical_and(leader, top_line))
    def _():
        mat_x[slab] = own

    send_a = [remote(mat_a.at[spot], mat_a.at[spot], rm_a.at[spot], in_plane(7))]
    send_z = [
        remote(mat_z.at[line], mat_z.at[line], rm_z.at[line], in_line(lax.rem(line + p, 8)))
        for p in FAR
    ]
    send_x = [
        remote(mat_x.at[slab], mat_x.at[slab], rm_x.at[slab], in_slab(lax.rem(slab + p, 4)))
        for p in (2, 1, 3)
    ]
    send_p = [remote(paths, paths, r_path, in_line(q)) for q in (3, 4, 2, 5, 1, 6, 0)]

    loads[2].wait()
    loads[3].wait()

    @pl.loop(0, NLEAF)
    def _(leaf):
        at = pl.multiple_of(leaf * LEAF, LEAF)
        dh, dl = split(d_in[:, pl.ds(at, LEAF)])
        bh, bl = split(b_in[:, pl.ds(at, LEAF)])
        both_d = jnp.concatenate([dh, dl], axis=0)
        both_b = jnp.concatenate([bh, bl], axis=0)
        d_split[:, pl.ds(at, LEAF)] = both_d
        b_split[:, pl.ds(at, LEAF)] = both_b
        prod = mxu(both_d, both_b, NT)
        leaf_c[leaf] = (prod[0:64, 0:64] + prod[64:128, 64:128]) + (prod[0:64, 64:128] + prod[64:128, 0:64])

    for k in range(4):
        leaf_c[8 + k] = raise_pair(t_in[2 * k], leaf_c[2 * k], leaf_c[2 * k + 1])
    for k in range(2):
        leaf_c[12 + k] = raise_pair(t_in[4 * k + 1], leaf_c[8 + 2 * k], leaf_c[9 + 2 * k])
    c_a[spot] = pack(raise_pair(t_in[3], leaf_c[12], leaf_c[13]))
    send_ca = [remote(c_a.at[spot], c_a.at[spot], rc_a.at[spot], in_plane(7))]
    owner = jnp.logical_and(jnp.logical_and(leader, top_line), slab < 3)
    pl.semaphore_wait(barrier, 17)
    @pl.when(jnp.logical_not(leader))
    def _():
        for copy in send_ca + send_a:
            copy.start()

    @pl.when(jnp.logical_and(leader, jnp.logical_not(top_line)))
    def _():
        for copy in send_z:
            copy.start()

    @pl.when(owner)
    def _():
        for copy in send_x:
            copy.start()

    local = lower_tree(lambda i: (t_in[i], k_in[i]), lambda i: leaf_c[i])
    local_f[...] = local[0:64]
    local_op[0], local_op[1] = split(local[64:128])

    loads[4].wait()
    loads[5].wait()

    @pl.loop(0, ROWS // 128)
    def _(i):
        at = pl.multiple_of(i * 128, 128)
        x_rows[pl.ds(at, 128), 0:64] = x_in[:, pl.ds(at, 128)].T * (ROOT_FIVE / LN_TWO * scale[...])

    def dense(first, last):
        @pl.loop(first, last)
        def _(leaf):
            at = pl.multiple_of(leaf * LEAF, LEAF)

            @pl.loop(0, LEAF // 32)
            def _(i):
                base = pl.multiple_of(i * 32, 32)
                for j in range(32):
                    x_perm[pl.ds(base + j, 1), :] = x_rows[pl.ds(perm[at + base + j], 1), :]

            xh, xl = split(x_perm[:, 0:64])
            near = xh.astype(F32) + xl.astype(F32)
            square = jnp.sum(near * near, axis=1, keepdims=True)
            square_row = jnp.broadcast_to(square, (LEAF, 128)).T[0:1]
            minus = jnp.asarray(-2.0, BF16)
            one = jnp.concatenate([xh * minus, xh * minus, xl * minus, xl * minus], axis=1)
            two = jnp.concatenate([xh, xl, xh, xl], axis=1)
            vectors = d_split[:, pl.ds(at, LEAF)]
            for c in range(0, LEAF, 256):
                inner = mxu(one, two[c : c + 256], NT)
                dist_sq = jnp.maximum((square + square_row[:, c : c + 256]) + inner, 1e-30)
                dist = dist_sq * lax.rsqrt(dist_sq)
                value = ((1.0 + dist * LN_TWO) + dist_sq * (LN_TWO * LN_TWO / 3.0)) * jnp.exp2(-dist)
                vh, vl = split(value)
                got = mxu(vectors, vh) + mxu(vectors, vl)
                image[:, pl.ds(at + c, 256)] = got[0:64] + got[64:128]

    def mats(ref):
        return ref[0:64, :], unpack(ref[64:96, :])

    def mats(ref):
        return ref[0:64, :], unpack(ref[64:96, :])

    dense(0, 0)

    @pl.when(jnp.logical_and(leader, top_line))
    def _():
        for q in range(3):
            @pl.when(slab != q)
            def _():
                arrived(mat_x.at[q], rm_x.at[q])
        half = lax.div(slab, 2)
        side = lax.rem(slab, 2)
        t, b = mats(mat_x.at[half * 2])
        beside = jnp.where(side == 0, b.T, b)
        turn = jnp.where(side == 0, t[:, 0:64], t[:, 64:128])
        t, b = mats(mat_x.at[1])
        across = product(jnp.where(half == 0, b.T, b), turn, NT)
        t, b = mats(mat_x.at[2 - half * 2])
        paths[...] = pack(
            jnp.concatenate([beside, product(t[:, 0:64], across), product(t[:, 64:128], across)], axis=0)
        )
        for copy in send_p:
            copy.start()

    dense(0, 1)

    send_cz = [
        remote(c_z.at[line], c_z.at[line], rc_z.at[line], in_line(lax.rem(line + p, 8)))
        for p in FAR
    ]
    send_cx = [
        remote(c_x.at[slab], c_x.at[slab], rc_x.at[slab], in_slab(lax.rem(slab + p, 4)))
        for p in (2, 1, 3)
    ]
    send_f = [remote(f_out.at[q], f_top, r_f, in_plane(q)) for q in range(7)]

    @pl.when(leader)
    def _():
        for q in range(7):
            arrived(c_a.at[q], rc_a.at[q])
            arrived(mat_a.at[q], rm_a.at[q])
        for k in range(8):
            pair_c[k] = unpack(c_a[k])
        for k in range(4):
            pair_c[8 + k] = raise_pair(mat_a[2 * k, 0:64, :], pair_c[2 * k], pair_c[2 * k + 1])
        for k in range(2):
            pair_c[12 + k] = raise_pair(mat_a[4 * k + 1, 0:64, :], pair_c[8 + 2 * k], pair_c[9 + 2 * k])
        c_z[line] = pack(raise_pair(mat_a[3, 0:64, :], pair_c[12], pair_c[13]))
        for copy in send_cz:
            copy.start()
        plane = lower_tree(lambda i: mats(mat_a.at[i]), lambda i: pair_c[i])
        plane_f[...] = plane[0:64]
        plane_op[...] = plane[64:128]

    dense(1, 3)

    @pl.when(leader)
    def _():
        for p in range(1, 8):
            q = lax.rem(line + p, 8)
            arrived(c_z.at[q], rc_z.at[q])

            @pl.when(q != 7)
            def _():
                arrived(mat_z.at[q], rm_z.at[q])
        for k in range(8):
            pair_c[k] = unpack(c_z[k])
        for k in range(4):
            pair_c[8 + k] = raise_pair(mat_z[2 * k, 0:64, :], pair_c[2 * k], pair_c[2 * k + 1])
        for k in range(2):
            pair_c[12 + k] = raise_pair(mat_z[4 * k + 1, 0:64, :], pair_c[8 + 2 * k], pair_c[9 + 2 * k])
        c_x[slab] = pack(raise_pair(mat_z[3, 0:64, :], pair_c[12], pair_c[13]))
        for copy in send_cx:
            copy.start()

        half = lax.div(line, 4)
        quarter = lax.div(line, 2)
        t, b = mats(mat_z.at[3])
        state = lower(half == 0, t, b, pair_c[13 - half], identity())
        side = lax.rem(quarter, 2)
        t, b = mats(mat_z.at[half * 4 + 1])
        state = lower(side == 0, t, b, pair_c[8 + half * 2 + 1 - side], state)
        side = lax.rem(line, 2)
        t, b = mats(mat_z.at[quarter * 2])
        state = lower(side == 0, t, b, pair_c[quarter * 2 + 1 - side], state)
        both = product(state, plane_op[...])
        plane_f[...] = plane_f[...] + both[0:64]

        @pl.when(jnp.logical_not(top_line))
        def _():
            arrived(paths, r_path)
        slab_op[0], slab_op[1] = split(product(unpack(paths[...]), both[64:128]))

    dense(3, 5)

    @pl.when(leader)
    def _():
        for p in range(1, 4):
            q = lax.rem(slab + p, 4)
            arrived(c_x.at[q], rc_x.at[q])
        half = lax.div(slab, 2)
        others = (half * 2 + 1 - lax.rem(slab, 2), 2 - half * 2, 3 - half * 2)
        ch, cl = split(jnp.concatenate([unpack(c_x[q]) for q in others], axis=1))
        far = plane_f[...] + (mxu(ch, slab_op[0]) + (mxu(ch, slab_op[1]) + mxu(cl, slab_op[0])))
        for q in range(8):
            f_out[q] = pack(far[:, q * 64 : q * 64 + 64])
        for copy in send_f:
            copy.start()
        f_top[...] = f_out[7]

    dense(5, 8)

    @pl.when(jnp.logical_not(leader))
    def _():
        arrived(f_top, r_f)
    fh, fl = split(unpack(f_top[...]))
    far = local_f[...] + (mxu(fh, local_op[0]) + (mxu(fh, local_op[1]) + mxu(fl, local_op[0])))
    for k in range(NLEAF):
        fh, fl = split(far[:, k * 64 : k * 64 + 64])
        leaf_f[k] = jnp.concatenate(
            [jnp.concatenate([fh, fh], axis=1), jnp.concatenate([fl, fl], axis=1)], axis=0
        )

    loads[6].wait()
    shift = noise[0]
    zero = jnp.zeros((COLS, 128), F32)

    def store(leaf):
        at = pl.multiple_of(leaf * LEAF, LEAF)
        return pltpu.make_async_copy(
            image.at[:, pl.ds(at, LEAF)], out_image.at[:, pl.ds(at, LEAF)], out_sem.at[leaf]
        )

    def add_leaf(leaf, sums):
        at = pl.multiple_of(leaf * LEAF, LEAF)
        far = mxu(leaf_f[leaf], b_split[:, pl.ds(at, LEAF)])
        d = d_in[:, pl.ds(at, LEAF)]
        r = r_in[:, pl.ds(at, LEAF)]
        q = image[:, pl.ds(at, LEAF)] + shift * d + (far[0:64] + far[64:128])
        image[:, pl.ds(at, LEAF)] = q
        store(leaf).start()
        terms = (r * r, d * q, r * q, q * q)
        return tuple(
            total + ((term[:, 0:128] + term[:, 128:256]) + (term[:, 256:384] + term[:, 384:512]))
            for total, term in zip(sums, terms)
        )

    sums = lax.fori_loop(0, NLEAF, add_leaf, (zero, zero, zero, zero))
    lane = lax.broadcasted_iota(jnp.int32, (COLS, 128), 1)
    table = zero
    for i, total in enumerate(sums):
        table = jnp.where(lane == i, jnp.sum(total, axis=1, keepdims=True), table)
    value = table.T[0:8, :]

    first = 0
    send_red = []
    for size, place, device in ((8, spot, in_plane), (8, line, in_line), (4, slab, in_slab)):
        reduce[first + place, :, 0:64] = value
        copies = []
        for p in FAR if size == 8 else (2, 1, 3):
            q = lax.rem(place + p, size)
            copies.append(
                remote(reduce.at[first + place], reduce.at[first + place], r_red.at[first + place], device(q))
            )
        for copy in copies:
            copy.start()
        send_red.extend(copies)
        for p in range(1, size):
            q = lax.rem(place + p, size)
            arrived(reduce.at[first + q], r_red.at[first + q])
        value = reduce[first, :, 0:64]
        for q in range(1, size):
            value = value + reduce[first + q, :, 0:64]
        first += size

    old, curve, cross, own_square = value[0:1], value[1:2], value[2:3], value[3:4]
    alpha = old / curve
    new = old - 2.0 * alpha * cross + alpha * alpha * own_square
    ratio = new / old
    out_coef[0] = jnp.broadcast_to(alpha, (128, COLS)).T
    out_coef[1] = jnp.broadcast_to(ratio, (128, COLS)).T

    for copy in send_red:
        copy.wait_send()

    @pl.when(jnp.logical_not(leader))
    def _():
        for copy in send_ca + send_a:
            copy.wait_send()

    @pl.when(leader)
    def _():
        for copy in send_cz + send_cx + send_f:
            copy.wait_send()

    @pl.when(jnp.logical_and(leader, jnp.logical_not(top_line)))
    def _():
        for copy in send_z:
            copy.wait_send()

    @pl.when(owner)
    def _():
        for copy in send_x:
            copy.wait_send()

    @pl.when(jnp.logical_and(leader, top_line))
    def _():
        for copy in send_p:
            copy.wait_send()

    @pl.loop(0, NLEAF)
    def _(leaf):
        store(leaf).wait()


def finish(coef, image, sol, res, direc, out_sol, out_res, out_dir, held, made, in_sem, out_sem):
    parts = in_sem.shape[1]
    width = ROWS // parts
    alpha = jnp.concatenate([coef[0]] * (width // 128), axis=1)
    ratio = jnp.concatenate([coef[1]] * (width // 128), axis=1)
    loads = [
        [
            pltpu.make_async_copy(
                src.at[:, pl.ds(k * width, width)], held.at[i, :, pl.ds(k * width, width)], in_sem.at[i, k]
            )
            for i, src in enumerate((image, sol, res, direc))
        ]
        for k in range(parts)
    ]
    stores = [
        [
            pltpu.make_async_copy(
                made.at[i, :, pl.ds(k * width, width)], dst.at[:, pl.ds(k * width, width)], out_sem.at[i, k]
            )
            for i, dst in enumerate((out_sol, out_res, out_dir))
        ]
        for k in range(parts)
    ]
    for part in loads:
        for load in part:
            load.start()
    for k in range(parts):
        for load in loads[k]:
            load.wait()
        at = pl.ds(k * width, width)
        d = held[3, :, at]
        r = held[2, :, at] - alpha * held[0, :, at]
        made[0, :, at] = held[1, :, at] + alpha * d
        made[1, :, at] = r
        made[2, :, at] = r + ratio * d
        for store in stores[k]:
            store.start()
    for part in stores:
        for store in part:
            store.wait()


def on_device(
    coords, perm, inv_scale, noise, leaf_basis, pair_transfer, coupling, solution, residual, direction
):
    hbm = pl.BlockSpec(memory_space=pltpu.HBM)
    anywhere = pl.BlockSpec(memory_space=pl.ANY)
    smem = pl.BlockSpec(memory_space=pltpu.SMEM)
    vmem = pl.BlockSpec(memory_space=pltpu.VMEM)
    wide = jax.ShapeDtypeStruct((COLS, ROWS), F32)
    dma = pltpu.SemaphoreType.DMA
    image, coef = pl.pallas_call(
        kernel,
        out_shape=(wide, jax.ShapeDtypeStruct((2, COLS, 128), F32)),
        in_specs=[hbm, hbm, vmem, smem, hbm, hbm, hbm, hbm, hbm],
        out_specs=(anywhere, vmem),
        scratch_shapes=[
            pltpu.SMEM((ROWS,), jnp.int32),
            pltpu.VMEM((64, ROWS), F32),
            pltpu.VMEM((ROWS, 128), F32),
            pltpu.VMEM((LEAF, 128), F32),
            pltpu.VMEM((64, ROWS), F32),
            pltpu.VMEM((8, 64, 128), F32),
            pltpu.VMEM((8, 64, 64), F32),
            pltpu.VMEM((64, ROWS), F32),
            pltpu.VMEM((64, ROWS), F32),
            pltpu.VMEM((64, ROWS), F32),
            pltpu.VMEM((128, ROWS), BF16),
            pltpu.VMEM((128, ROWS), BF16),
            pltpu.VMEM((14, 64, 64), F32),
            pltpu.VMEM((8, 128, 128), BF16),
            pltpu.VMEM((8, 96, 128), F32),
            pltpu.VMEM((8, 96, 128), F32),
            pltpu.VMEM((4, 96, 128), F32),
            pltpu.VMEM((96, 128), F32),
            pltpu.VMEM((8, 32, 128), F32),
            pltpu.VMEM((8, 32, 128), F32),
            pltpu.VMEM((4, 32, 128), F32),
            pltpu.VMEM((32, 128), F32),
            pltpu.VMEM((8, 32, 128), F32),
            pltpu.VMEM((14, 64, 64), F32),
            pltpu.VMEM((20, 8, 128), F32),
            pltpu.VMEM((64, LEAF), F32),
            pltpu.VMEM((2, 64, LEAF), BF16),
            pltpu.VMEM((64, LEAF), F32),
            pltpu.VMEM((64, LEAF), F32),
            pltpu.VMEM((2, 192, LEAF), BF16),
            dma((7,)),
            dma((NLEAF,)),
            dma((96,)),
            dma((8,)),
            dma((8,)),
            dma((4,)),
            dma,
            dma((8,)),
            dma((8,)),
            dma((4,)),
            dma,
            dma((20,)),
        ],
        compiler_params=pltpu.CompilerParams(
            collective_id=0, has_side_effects=True, vmem_limit_bytes=60 * 2**20
        ),
        cost_estimate=pl.CostEstimate(flops=4 * 10**9, bytes_accessed=10 * 2**20, transcendentals=4 * 2**20),
        name="cg_step",
    )(
        coords.T, perm, inv_scale.reshape(1, 64), noise, leaf_basis.T, pair_transfer, coupling,
        residual.T, direction.T,
    )
    parts = 4
    outs = pl.pallas_call(
        finish,
        out_shape=(wide, wide, wide),
        in_specs=[vmem, anywhere, anywhere, anywhere, anywhere],
        out_specs=(anywhere, anywhere, anywhere),
        scratch_shapes=[
            pltpu.VMEM((4, COLS, ROWS), F32),
            pltpu.VMEM((3, COLS, ROWS), F32),
            dma((4, parts)),
            dma((3, parts)),
        ],
        compiler_params=pltpu.CompilerParams(vmem_limit_bytes=60 * 2**20),
        name="cg_finish",
    )(coef, image, solution.T, residual.T, direction.T)
    return tuple(out.T for out in outs)


def solution(mesh):
    rows = P(("group", "within"), None)
    cubes = P(("group", "within"), None, None)
    in_specs = (rows, P(("group", "within")), P(), P(), rows, cubes, cubes, rows, rows, rows)
    return jax.shard_map(
        on_device, mesh=mesh, in_specs=in_specs, out_specs=(rows, rows, rows), check_vma=False
    )
```

time: 61.2 us -> 53.7 us (0.88)
  local copies, waits for them, and re-layouts: 6.18 us -> 0 us
  Pallas kernels: 53.5 us -> 52 us
    unnamed x11 -> x0, local copies, waits for them, and re-layouts: 6.18 us -> none
    pallas_call x1 -> x2, Pallas kernels: 53.5 us -> 52 us  [the longest x1 47.8 us: on_device(): pl.pallas_call(kernel, out_shape=(wide, jax.ShapeDtypeStruct((2, COLS, 12...]
where the time goes in v2:
time: 53.7 us; the launch traced here: 53.3 us
  Pallas kernels  52 us (97%)
  between operations  1.29 us (2%)
    pallas_call x1, Pallas kernels, on_device(): pl.pallas_call(kernel, out_shape=(wide, jax.ShapeDtypeStruct((2, COLS, 12...  47.8 us
    pallas_call x1, Pallas kernels, on_device(): pl.pallas_call(finish, out_shape=(wide, wide, wide), in_specs=[vmem, anyw...  4.17 us

profile of v2, /device:TPU:1, one launch (start us, length us, event | category | flops | bytes accessed | tf_op | source)
XLA Modules:
  0.0 53.3 jit_solution(8666629144225049509)
XLA Ops:
  1.3 47.8 %cg_step.1 = (f32[64,4096]{1,0:T(8,128)}, f32[2,64,128]{2,1,0:T(8,128)}) custom-call(f32[64,4096]{1,0:T(8,128)} %bitcast.14, s32[4096]{0:T(1024)} %order.1, f32[1,64]{1,0:T(1,128)} %bitcast.19, f32[1]{0:T(128)S(6)} %copy.13.noise, f32[64,4096]{1,0:T(8,128)} %bitcast.15, f32[8,64,128]{2,1,0:T(8,128)} %transfer.1, f32[8,64,64]{2,1,0:T(8,128)} %coupling.1, ...), custom_call_target="tpu_custom_call" | custom-call | flops 4000000000 | bytes 10485760 | tf_op jit(solution)/shard_map/cg_step/pallas_call | solution.py:529
  49.1 4.2 %cg_finish.1 = (f32[64,4096]{1,0:T(8,128)}, f32[64,4096]{1,0:T(8,128)}, f32[64,4096]{1,0:T(8,128)}) custom-call(f32[2,64,128]{2,1,0:T(8,128)} %get-tuple-element.8.coef, f32[64,4096]{1,0:T(8,128)} %get-tuple-element.9.image, f32[64,4096]{1,0:T(8,128)} %bitcast.13, f32[64,4096]{1,0:T(8,128)} %bitcast.10, f32[64,4096]{1,0:T(8,128)} %bitcast.12), custom_call_target="tpu_custom_call" | custom-call | tf_op jit(solution)/shard_map/cg_finish/pallas_call | solution.py:588

commit v3 on v2

--- a/solution.py
+++ b/solution.py
@@ -35,7 +35,9 @@
 def product(a, b, dims=NN):
     ah, al = split(a)
     bh, bl = split(b)
-    return mxu(ah, bh, dims) + (mxu(ah, bl, dims) + mxu(al, bh, dims))
+    axis = 1 if dims == NT else 0
+    both = mxu(jnp.concatenate([ah, al], axis=1), jnp.concatenate([bh, bh], axis=axis), dims)
+    return both + mxu(ah, bl, dims)
 
 
 def pack(c):
@@ -216,10 +218,6 @@
         for copy in send_x:
             copy.start()
 
-    local = lower_tree(lambda i: (t_in[i], k_in[i]), lambda i: leaf_c[i])
-    local_f[...] = local[0:64]
-    local_op[0], local_op[1] = split(local[64:128])
-
     loads[4].wait()
     loads[5].wait()
 
@@ -228,16 +226,20 @@
         at = pl.multiple_of(i * 128, 128)
         x_rows[pl.ds(at, 128), 0:64] = x_in[:, pl.ds(at, 128)].T * (ROOT_FIVE / LN_TWO * scale[...])
 
+    def gather(at, first, count):
+        for j in range(first, first + count):
+            x_perm[pl.ds(j, 1), :] = x_rows[pl.ds(perm[at + j], 1), :]
+
+    @pl.loop(0, LEAF // 64)
+    def _(i):
+        base = pl.multiple_of(i * 64, 64)
+        for j in range(64):
+            x_perm[pl.ds(base + j, 1), :] = x_rows[pl.ds(perm[base + j], 1), :]
+
     def dense(first, last):
         @pl.loop(first, last)
         def _(leaf):
             at = pl.multiple_of(leaf * LEAF, LEAF)
-
-            @pl.loop(0, LEAF // 32)
-            def _(i):
-                base = pl.multiple_of(i * 32, 32)
-                for j in range(32):
-                    x_perm[pl.ds(base + j, 1), :] = x_rows[pl.ds(perm[at + base + j], 1), :]
 
             xh, xl = split(x_perm[:, 0:64])
             near = xh.astype(F32) + xl.astype(F32)
@@ -247,14 +249,16 @@
             one = jnp.concatenate([xh * minus, xh * minus, xl * minus, xl * minus], axis=1)
             two = jnp.concatenate([xh, xl, xh, xl], axis=1)
             vectors = d_split[:, pl.ds(at, LEAF)]
+            following = jnp.minimum(at + LEAF, ROWS - LEAF)
             for c in range(0, LEAF, 256):
+                gather(following, c, 256)
                 inner = mxu(one, two[c : c + 256], NT)
                 dist_sq = jnp.maximum((square + square_row[:, c : c + 256]) + inner, 1e-30)
                 dist = dist_sq * lax.rsqrt(dist_sq)
                 value = ((1.0 + dist * LN_TWO) + dist_sq * (LN_TWO * LN_TWO / 3.0)) * jnp.exp2(-dist)
                 vh, vl = split(value)
-                got = mxu(vectors, vh) + mxu(vectors, vl)
-                image[:, pl.ds(at + c, 256)] = got[0:64] + got[64:128]
+                got = mxu(vectors, vh)
+                image[:, pl.ds(at + c, 256)] = got[0:64] + (got[64:128] + mxu(vectors[0:64], vl))
 
     def mats(ref):
         return ref[0:64, :], unpack(ref[64:96, :])
@@ -314,7 +318,7 @@
         plane_f[...] = plane[0:64]
         plane_op[...] = plane[64:128]
 
-    dense(1, 3)
+    dense(1, 4)
 
     @pl.when(leader)
     def _():
@@ -353,7 +357,7 @@
             arrived(paths, r_path)
         slab_op[0], slab_op[1] = split(product(unpack(paths[...]), both[64:128]))
 
-    dense(3, 5)
+    dense(4, 6)
 
     @pl.when(leader)
     def _():
@@ -370,7 +374,11 @@
             copy.start()
         f_top[...] = f_out[7]
 
-    dense(5, 8)
+    local = lower_tree(lambda i: (t_in[i], k_in[i]), lambda i: leaf_c[i])
+    local_f[...] = local[0:64]
+    local_op[0], local_op[1] = split(local[64:128])
+
+    dense(6, 8)
 
     @pl.when(jnp.logical_not(leader))
     def _():

time: 53.7 us -> 50.8 us (0.946)
  Pallas kernels: 52 us -> 49.3 us
    pallas_call x1, Pallas kernels: 47.8 us -> 45.2 us  [on_device(): pl.pallas_call(kernel, out_shape=(wide, jax.ShapeDtypeStruct((2, COLS, 12...]
where the time goes in v3:
time: 50.8 us; the launch traced here: 50.6 us
  Pallas kernels  49.3 us (97%)
  between operations  1.29 us (3%)
    pallas_call x1, Pallas kernels, on_device(): pl.pallas_call(kernel, out_shape=(wide, jax.ShapeDtypeStruct((2, COLS, 12...  45.2 us
    pallas_call x1, Pallas kernels, on_device(): pl.pallas_call(finish, out_shape=(wide, wide, wide), in_specs=[vmem, anyw...  4.17 us

profile of v3, /device:TPU:1, one launch (start us, length us, event | category | flops | bytes accessed | tf_op | source)
XLA Modules:
  0.0 50.6 jit_solution(10363800660348980256)
XLA Ops:
  1.3 45.2 %cg_step.1 = (f32[64,4096]{1,0:T(8,128)}, f32[2,64,128]{2,1,0:T(8,128)}) custom-call(f32[64,4096]{1,0:T(8,128)} %bitcast.14, s32[4096]{0:T(1024)} %order.1, f32[1,64]{1,0:T(1,128)} %bitcast.19, f32[1]{0:T(128)S(6)} %copy.13.noise, f32[64,4096]{1,0:T(8,128)} %bitcast.15, f32[8,64,128]{2,1,0:T(8,128)} %transfer.1, f32[8,64,64]{2,1,0:T(8,128)} %coupling.1, ...), custom_call_target="tpu_custom_call" | custom-call | flops 4000000000 | bytes 10485760 | tf_op jit(solution)/shard_map/cg_step/pallas_call | solution.py:537
  46.4 4.2 %cg_finish.1 = (f32[64,4096]{1,0:T(8,128)}, f32[64,4096]{1,0:T(8,128)}, f32[64,4096]{1,0:T(8,128)}) custom-call(f32[2,64,128]{2,1,0:T(8,128)} %get-tuple-element.8.coef, f32[64,4096]{1,0:T(8,128)} %get-tuple-element.9.image, f32[64,4096]{1,0:T(8,128)} %bitcast.13, f32[64,4096]{1,0:T(8,128)} %bitcast.10, f32[64,4096]{1,0:T(8,128)} %bitcast.12), custom_call_target="tpu_custom_call" | custom-call | tf_op jit(solution)/shard_map/cg_finish/pallas_call | solution.py:596

commit v4 on v3

--- a/solution.py
+++ b/solution.py
@@ -91,11 +91,11 @@
 
 def kernel(
     coords, order, scale, noise, basis, transfer, coupling, res, direc,
-    out_image, out_coef,
+    out_image,
     perm, x_in, x_rows, x_perm, b_in, t_in, k_in, r_in, d_in, image,
     d_split, b_split, leaf_c, leaf_f,
     mat_a, mat_z, mat_x, paths, c_a, c_z, c_x, f_top, f_out, pair_c, reduce,
-    local_f, local_op, plane_f, plane_op, slab_op,
+    local_f, local_op, plane_f, plane_op, slab_op, coef,
     in_sem, out_sem, send_sem, rm_a, rm_z, rm_x, r_path, rc_a, rc_z, rc_x, r_f, r_red,
 ):
     group = lax.axis_index("group")
@@ -447,8 +447,10 @@
     alpha = old / curve
     new = old - 2.0 * alpha * cross + alpha * alpha * own_square
     ratio = new / old
-    out_coef[0] = jnp.broadcast_to(alpha, (128, COLS)).T
-    out_coef[1] = jnp.broadcast_to(ratio, (128, COLS)).T
+    coef[:, 0:128] = jnp.broadcast_to(alpha, (128, COLS)).T
+    coef[:, 128:256] = jnp.broadcast_to(ratio, (128, COLS)).T
+    store_coef = pltpu.make_async_copy(coef, out_image.at[:, pl.ds(ROWS, 256)], out_sem.at[NLEAF])
+    store_coef.start()
 
     for copy in send_red:
         copy.wait_send()
@@ -482,12 +484,14 @@
     def _(leaf):
         store(leaf).wait()
 
-
-def finish(coef, image, sol, res, direc, out_sol, out_res, out_dir, held, made, in_sem, out_sem):
+    store_coef.wait()
+
+
+def finish(image, sol, res, direc, out_sol, out_res, out_dir, held, made, coef, in_sem, out_sem):
     parts = in_sem.shape[1]
     width = ROWS // parts
-    alpha = jnp.concatenate([coef[0]] * (width // 128), axis=1)
-    ratio = jnp.concatenate([coef[1]] * (width // 128), axis=1)
+    load_coef = pltpu.make_async_copy(image.at[:, pl.ds(ROWS, 256)], coef, in_sem.at[4, 0])
+    load_coef.start()
     loads = [
         [
             pltpu.make_async_copy(
@@ -509,6 +513,9 @@
     for part in loads:
         for load in part:
             load.start()
+    load_coef.wait()
+    alpha = jnp.concatenate([coef[:, 0:128]] * (width // 128), axis=1)
+    ratio = jnp.concatenate([coef[:, 128:256]] * (width // 128), axis=1)
     for k in range(parts):
         for load in loads[k]:
             load.wait()
@@ -534,11 +541,11 @@
     vmem = pl.BlockSpec(memory_space=pltpu.VMEM)
     wide = jax.ShapeDtypeStruct((COLS, ROWS), F32)
     dma = pltpu.SemaphoreType.DMA
-    image, coef = pl.pallas_call(
+    image = pl.pallas_call(
         kernel,
-        out_shape=(wide, jax.ShapeDtypeStruct((2, COLS, 128), F32)),
+        out_shape=jax.ShapeDtypeStruct((COLS, ROWS + 256), F32),
         in_specs=[hbm, hbm, vmem, smem, hbm, hbm, hbm, hbm, hbm],
-        out_specs=(anywhere, vmem),
+        out_specs=anywhere,
         scratch_shapes=[
             pltpu.SMEM((ROWS,), jnp.int32),
             pltpu.VMEM((64, ROWS), F32),
@@ -570,8 +577,9 @@
             pltpu.VMEM((64, LEAF), F32),
             pltpu.VMEM((64, LEAF), F32),
             pltpu.VMEM((2, 192, LEAF), BF16),
+            pltpu.VMEM((COLS, 256), F32),
             dma((7,)),
-            dma((NLEAF,)),
+            dma((NLEAF + 1,)),
             dma((96,)),
             dma((8,)),
             dma((8,)),
@@ -596,17 +604,18 @@
     outs = pl.pallas_call(
         finish,
         out_shape=(wide, wide, wide),
-        in_specs=[vmem, anywhere, anywhere, anywhere, anywhere],
+        in_specs=[anywhere, anywhere, anywhere, anywhere],
         out_specs=(anywhere, anywhere, anywhere),
         scratch_shapes=[
             pltpu.VMEM((4, COLS, ROWS), F32),
             pltpu.VMEM((3, COLS, ROWS), F32),
-            dma((4, parts)),
+            pltpu.VMEM((COLS, 256), F32),
+            dma((5, parts)),
             dma((3, parts)),
         ],
-        compiler_params=pltpu.CompilerParams(vmem_limit_bytes=60 * 2**20),
+        compiler_params=pltpu.CompilerParams(vmem_limit_bytes=12 * 2**20),
         name="cg_finish",
-    )(coef, image, solution.T, residual.T, direction.T)
+    )(image, solution.T, residual.T, direction.T)
     return tuple(out.T for out in outs)
 
 

time: 50.8 us -> 50.3 us (level)
  Pallas kernels: 49.3 us -> 47.5 us
  local copies, waits for them, and re-layouts: 0 us -> 1.25 us
    pallas_call x2, Pallas kernels: 49.3 us -> 47.5 us  [the longest x1 45.2 us: on_device(): pl.pallas_call(kernel, out_shape=jax.ShapeDtypeStruct((COLS, ROWS + 256),...]
    unnamed x0 -> x8, local copies, waits for them, and re-layouts: none -> 1.25 us
where the time goes in v4:
time: 50.3 us; the launch traced here: 50.1 us
  Pallas kernels  47.5 us (94%)
  between operations  1.34 us (3%)
  local copies, waits for them, and re-layouts  1.25 us (2%)
    pallas_call x1, Pallas kernels, on_device(): pl.pallas_call(kernel, out_shape=jax.ShapeDtypeStruct((COLS, ROWS + 256),...  45.2 us
    pallas_call x1, Pallas kernels, on_device(): pl.pallas_call(finish, out_shape=(wide, wide, wide), in_specs=[anywhere,...  2.31 us
    unnamed x8, local copies, waits for them, and re-layouts  1.25 us

profile of v4, /device:TPU:1, one launch (start us, length us, event | category | flops | bytes accessed | tf_op | source)
XLA Modules:
  0.0 50.1 jit_solution(5514831853198815495)
XLA Ops:
  1.3 0.0 copy-start.1
  1.3 0.0 copy-start.2
  1.3 0.0 copy-start.3
  1.3 45.2 %cg_step.1.image = f32[64,4352]{1,0:T(8,128)} custom-call(f32[64,4096]{1,0:T(8,128)} %bitcast.14, s32[4096]{0:T(1024)} %order.1, f32[1,64]{1,0:T(1,128)} %bitcast.19, f32[1]{0:T(128)S(6)} %copy.13.noise, f32[64,4096]{1,0:T(8,128)} %bitcast.15, f32[8,64,128]{2,1,0:T(8,128)} %transfer.1, f32[8,64,64]{2,1,0:T(8,128)} %coupling.1, f32[64,4096]{1,0:T(8,128)} %bitcast.9, ...), custom_call_target="tpu_custom_call" | custom-call | flops 4000000000 | bytes 10485760 | tf_op jit(solution)/shard_map/cg_step/pallas_call | solution.py:544
  46.5 0.0 copy-done.1
  46.6 0.0 copy-done.2
  46.6 0.0 copy-done.3
  46.6 0.0 copy-start
  46.6 1.2 %copy-done = f32[64,4352]{1,0:T(8,128)S(1)} copy-done((f32[64,4352]{1,0:T(8,128)S(1)}, f32[64,4352]{1,0:T(8,128)}, u32[]{:S(2)}) %copy-start) | copy-done | bytes 1114136
  47.8 2.3 %cg_finish.1 = (f32[64,4096]{1,0:T(8,128)}, f32[64,4096]{1,0:T(8,128)}, f32[64,4096]{1,0:T(8,128)}) custom-call(f32[64,4352]{1,0:T(8,128)S(1)} %copy-done, f32[64,4096]{1,0:T(8,128)S(1)} %bitcast.13, f32[64,4096]{1,0:T(8,128)S(1)} %bitcast.10, f32[64,4096]{1,0:T(8,128)S(1)} %bitcast.12), custom_call_target="tpu_custom_call" | custom-call | tf_op jit(solution)/shard_map/cg_finish/pallas_call | solution.py:604
Async XLA Ops:
  1.3 45.3 %copy-start.1 = (f32[4096,64]{0,1:T(8,128)S(1)}, f32[4096,64]{0,1:T(8,128)}, u32[]{:S(2)}) copy-start(f32[4096,64]{0,1:T(8,128)} %param.18) | copy-start | bytes 3145732
  1.3 45.3 %copy-start.2 = (f32[4096,64]{0,1:T(8,128)S(1)}, f32[4096,64]{0,1:T(8,128)}, u32[]{:S(2)}) copy-start(f32[4096,64]{0,1:T(8,128)} %param.19) | copy-start | bytes 3145732
  1.3 45.3 %copy-start.3 = (f32[4096,64]{0,1:T(8,128)S(1)}, f32[4096,64]{0,1:T(8,128)}, u32[]{:S(2)}) copy-start(f32[4096,64]{0,1:T(8,128)} %param.17) | copy-start | bytes 3145732
  46.6 1.2 %copy-start = (f32[64,4352]{1,0:T(8,128)S(1)}, f32[64,4352]{1,0:T(8,128)}, u32[]{:S(2)}) copy-start(f32[64,4352]{1,0:T(8,128)} %cg_step.1.image) | copy-start | bytes 3342340

commit v5 on v4

--- a/solution.py
+++ b/solution.py
@@ -487,49 +487,25 @@
     store_coef.wait()
 
 
-def finish(image, sol, res, direc, out_sol, out_res, out_dir, held, made, coef, in_sem, out_sem):
-    parts = in_sem.shape[1]
+def finish(image, sol, res, direc, out_sol, out_res, out_dir, made, out_sem):
+    parts = out_sem.shape[1]
     width = ROWS // parts
-    load_coef = pltpu.make_async_copy(image.at[:, pl.ds(ROWS, 256)], coef, in_sem.at[4, 0])
-    load_coef.start()
-    loads = [
-        [
-            pltpu.make_async_copy(
-                src.at[:, pl.ds(k * width, width)], held.at[i, :, pl.ds(k * width, width)], in_sem.at[i, k]
-            )
-            for i, src in enumerate((image, sol, res, direc))
-        ]
-        for k in range(parts)
-    ]
-    stores = [
-        [
-            pltpu.make_async_copy(
-                made.at[i, :, pl.ds(k * width, width)], dst.at[:, pl.ds(k * width, width)], out_sem.at[i, k]
-            )
-            for i, dst in enumerate((out_sol, out_res, out_dir))
-        ]
-        for k in range(parts)
-    ]
-    for part in loads:
-        for load in part:
-            load.start()
-    load_coef.wait()
-    alpha = jnp.concatenate([coef[:, 0:128]] * (width // 128), axis=1)
-    ratio = jnp.concatenate([coef[:, 128:256]] * (width // 128), axis=1)
+    alpha = jnp.concatenate([image[:, ROWS : ROWS + 128]] * (width // 128), axis=1)
+    ratio = jnp.concatenate([image[:, ROWS + 128 : ROWS + 256]] * (width // 128), axis=1)
+    stores = []
     for k in range(parts):
-        for load in loads[k]:
-            load.wait()
         at = pl.ds(k * width, width)
-        d = held[3, :, at]
-        r = held[2, :, at] - alpha * held[0, :, at]
-        made[0, :, at] = held[1, :, at] + alpha * d
+        d = direc[:, at]
+        r = res[:, at] - alpha * image[:, at]
+        made[0, :, at] = sol[:, at] + alpha * d
         made[1, :, at] = r
         made[2, :, at] = r + ratio * d
-        for store in stores[k]:
+        for i, dst in enumerate((out_sol, out_res, out_dir)):
+            store = pltpu.make_async_copy(made.at[i, :, at], dst.at[:, at], out_sem.at[i, k])
             store.start()
-    for part in stores:
-        for store in part:
-            store.wait()
+            stores.append(store)
+    for store in stores:
+        store.wait()
 
 
 def on_device(
@@ -604,13 +580,10 @@
     outs = pl.pallas_call(
         finish,
         out_shape=(wide, wide, wide),
-        in_specs=[anywhere, anywhere, anywhere, anywhere],
+        in_specs=[vmem, vmem, vmem, vmem],
         out_specs=(anywhere, anywhere, anywhere),
         scratch_shapes=[
-            pltpu.VMEM((4, COLS, ROWS), F32),
             pltpu.VMEM((3, COLS, ROWS), F32),
-            pltpu.VMEM((COLS, 256), F32),
-            dma((5, parts)),
             dma((3, parts)),
         ],
         compiler_params=pltpu.CompilerParams(vmem_limit_bytes=12 * 2**20),

time: 50.3 us -> 49.8 us (0.990)
  no operation moved by 1% of the time
where the time goes in v5:
time: 49.8 us; the launch traced here: 49.7 us
  Pallas kernels  47.1 us (95%)
  between operations  1.34 us (3%)
  local copies, waits for them, and re-layouts  1.25 us (3%)
    pallas_call x1, Pallas kernels, on_device(): pl.pallas_call(kernel, out_shape=jax.ShapeDtypeStruct((COLS, ROWS + 256),...  45.2 us
    pallas_call x1, Pallas kernels, on_device(): pl.pallas_call(finish, out_shape=(wide, wide, wide), in_specs=[vmem, vmem...  1.83 us
    unnamed x8, local copies, waits for them, and re-layouts  1.25 us

profile of v5, /device:TPU:1, one launch (start us, length us, event | category | flops | bytes accessed | tf_op | source)
XLA Modules:
  0.0 49.7 jit_solution(7527892977941825127)
XLA Ops:
  1.3 0.0 copy-start.1
  1.3 0.0 copy-start.2
  1.3 0.0 copy-start.3
  1.3 45.2 %cg_step.1.image = f32[64,4352]{1,0:T(8,128)} custom-call(f32[64,4096]{1,0:T(8,128)} %bitcast.14, s32[4096]{0:T(1024)} %order.1, f32[1,64]{1,0:T(1,128)} %bitcast.19, f32[1]{0:T(128)S(6)} %copy.13.noise, f32[64,4096]{1,0:T(8,128)} %bitcast.15, f32[8,64,128]{2,1,0:T(8,128)} %transfer.1, f32[8,64,64]{2,1,0:T(8,128)} %coupling.1, f32[64,4096]{1,0:T(8,128)} %bitcast.9, ...), custom_call_target="tpu_custom_call" | custom-call | flops 4000000000 | bytes 10485760 | tf_op jit(solution)/shard_map/cg_step/pallas_call | solution.py:520
  46.5 0.0 copy-done.1
  46.6 0.0 copy-done.2
  46.6 0.0 copy-done.3
  46.6 0.0 copy-start
  46.6 1.2 %copy-done = f32[64,4352]{1,0:T(8,128)S(1)} copy-done((f32[64,4352]{1,0:T(8,128)S(1)}, f32[64,4352]{1,0:T(8,128)}, u32[]{:S(2)}) %copy-start) | copy-done | bytes 1114136
  47.8 1.8 %cg_finish.1 = (f32[64,4096]{1,0:T(8,128)}, f32[64,4096]{1,0:T(8,128)}, f32[64,4096]{1,0:T(8,128)}) custom-call(f32[64,4352]{1,0:T(8,128)S(1)} %copy-done, f32[64,4096]{1,0:T(8,128)S(1)} %bitcast.13, f32[64,4096]{1,0:T(8,128)S(1)} %bitcast.10, f32[64,4096]{1,0:T(8,128)S(1)} %bitcast.12), custom_call_target="tpu_custom_call" | custom-call | tf_op jit(solution)/shard_map/cg_finish/pallas_call | solution.py:580
Async XLA Ops:
  1.3 45.3 %copy-start.1 = (f32[4096,64]{0,1:T(8,128)S(1)}, f32[4096,64]{0,1:T(8,128)}, u32[]{:S(2)}) copy-start(f32[4096,64]{0,1:T(8,128)} %param.18) | copy-start | bytes 3145732
  1.3 45.3 %copy-start.2 = (f32[4096,64]{0,1:T(8,128)S(1)}, f32[4096,64]{0,1:T(8,128)}, u32[]{:S(2)}) copy-start(f32[4096,64]{0,1:T(8,128)} %param.19) | copy-start | bytes 3145732
  1.3 45.3 %copy-start.3 = (f32[4096,64]{0,1:T(8,128)S(1)}, f32[4096,64]{0,1:T(8,128)}, u32[]{:S(2)}) copy-start(f32[4096,64]{0,1:T(8,128)} %param.17) | copy-start | bytes 3145732
  46.6 1.2 %copy-start = (f32[64,4352]{1,0:T(8,128)S(1)}, f32[64,4352]{1,0:T(8,128)}, u32[]{:S(2)}) copy-start(f32[64,4352]{1,0:T(8,128)} %cg_step.1.image) | copy-start | bytes 3342340
